TPU v7x, 768 devices: a whole 4x8x12 slice. The times are simulated.
768 devices in a mesh: segment: 96 (over z_lo, y, x), head: 8 (over z_hi, core).
Axes of the slice: x: 4, y: 8, z: 12 (z_hi: 4, z_lo: 3; z = z_hi * 3 + z_lo), core: 2. Of those that a mesh axis runs over, the one named last changes fastest.
Arguments:
- grad_in: float32 [96, 128, 512], P('segment'), may hold values from -6 to 6
- memory: bfloat16 [96, 128, 512], P('segment'), may hold values from -120 to 120
- enc_grad_in: float32 [96, 128, 512], P('segment', None, 'head'), may hold values from -3 to 3
- act_stash: bfloat16 [96, 3, 128, 512], P('segment'), may hold values from -120 to 120
- slot_order: int32 [96, 3], P('segment'), may hold values from 0 to 2, each once within a row
- lengths: int32 [96, 3], P('segment'), may hold values from 16 to 128, as said below
- w_query: bfloat16 [96, 512, 8192], P('segment', None, 'head'), may hold values from -0.0234375 to 0.0234375
- w_key: bfloat16 [96, 512, 8192], P('segment', None, 'head'), may hold values from -0.25 to 0.25
- w_value: bfloat16 [96, 512, 8192], P('segment', None, 'head'), may hold values from -0.25 to 0.25
- w_out: bfloat16 [96, 8192, 512], P('segment', 'head'), may hold values from -0.0625 to 0.0625
Outputs:
- grad_out: float32 [96, 128, 512], P('segment')
- enc_grad_out: float32 [96, 128, 512], P('segment', None, 'head')
Inputs may be any that keep to these rules, and one draw needn't show every extreme that they name: `slot_order`: each row lists every stash slot once. `lengths`: some entry equals 128.
All inputs are finite; a program needn't handle non-finite values.
Results may differ from a plain program's by a relative error of at most 0.018.
The roundings to bfloat16 on the way count: a program that leaves them out, or rounds other values in their place, can miss the bound.
Values may be sent and summed in bfloat16 or wider, within the bound.
A program may use at most 32 MiB of HBM per device.

v0:
```python
import jax
import jax.numpy as jnp
from jax import lax
from jax.sharding import PartitionSpec as P

HEAD_DIM = 128
TICKS = 3


def copy_for_each(shard, axis):
    length = lax.axis_size(axis)
    return lax.all_to_all(
        jnp.broadcast_to(shard[None], (length, *shard.shape)), axis, 0, 0, tiled=True
    )


def in_order(pieces, dim):
    pieces = jnp.moveaxis(pieces, 0, dim)
    lengths = pieces.shape
    return pieces.reshape(*lengths[:dim], lengths[dim] * lengths[dim + 1], *lengths[dim + 2 :])


def gathered_copies(shard, axis, dim):
    pieces = copy_for_each(shard, axis)
    return in_order(pieces, dim)


def cut_along(shard, dim, length):
    before, after = (shard.shape[:dim], shard.shape[dim + 1 :])
    return jnp.moveaxis(shard.reshape(*before, length, -1, *after), dim, 0)


def sent_and_summed(shard, axis, dim):
    pieces = cut_along(shard, dim, lax.axis_size(axis))
    arrived = lax.all_to_all(pieces, axis, split_axis=0, concat_axis=0, tiled=True)
    return arrived.sum(axis=0)


def shifted(value, axis, steps):
    count = lax.axis_size(axis)
    pairs = [(source, (source + steps) % count) for source in range(count)]
    return lax.ppermute(value, axis, pairs)


def local_terms(
    gradient_low, held, decoded, length, query_weight, key_weight, value_weight, out_weight
):
    inner = query_weight.shape[1]
    head_local = inner // HEAD_DIM
    dec_rows = decoded.shape[0]
    enc_rows = held.shape[0]
    queries = jnp.dot(decoded, query_weight, preferred_element_type=jnp.float32).astype(
        jnp.bfloat16
    )
    keys = jnp.dot(held, key_weight, preferred_element_type=jnp.float32).astype(jnp.bfloat16)
    values = jnp.dot(held, value_weight, preferred_element_type=jnp.float32).astype(jnp.bfloat16)
    query_heads = queries.reshape(dec_rows, head_local, HEAD_DIM)
    key_heads = keys.reshape(enc_rows, head_local, HEAD_DIM)
    value_heads = values.reshape(enc_rows, head_local, HEAD_DIM)
    scores = jnp.einsum("qhd,khd->hqk", query_heads, key_heads, preferred_element_type=jnp.float32)
    allowed = lax.broadcasted_iota(jnp.int32, (1, 1, enc_rows), 2) < length
    scores = jnp.where(allowed, scores, jnp.float32(-1e30))
    row_max = jnp.max(scores, axis=-1, keepdims=True)
    expo = jnp.exp(scores - row_max)
    attention = expo / jnp.sum(expo, axis=-1, keepdims=True)
    attention_low = attention.astype(jnp.bfloat16)
    context_grad = jnp.einsum(
        "qe,ie->qi", gradient_low, out_weight, preferred_element_type=jnp.float32
    ).astype(jnp.bfloat16)
    context_heads = context_grad.reshape(dec_rows, head_local, HEAD_DIM)
    prob_grad = jnp.einsum(
        "qhd,khd->hqk", context_heads, value_heads, preferred_element_type=jnp.float32
    )
    score_grad = (
        attention * (prob_grad - jnp.sum(attention * prob_grad, axis=-1, keepdims=True))
    ).astype(jnp.bfloat16)
    query_grad = (
        jnp.einsum("hqk,khd->qhd", score_grad, key_heads, preferred_element_type=jnp.float32)
        .astype(jnp.bfloat16)
        .reshape(dec_rows, inner)
    )
    key_grad = (
        jnp.einsum("hqk,qhd->khd", score_grad, query_heads, preferred_element_type=jnp.float32)
        .astype(jnp.bfloat16)
        .reshape(enc_rows, inner)
    )
    value_grad = (
        jnp.einsum("hqk,qhd->khd", attention_low, context_heads, preferred_element_type=jnp.float32)
        .astype(jnp.bfloat16)
        .reshape(enc_rows, inner)
    )
    decoder_part = jnp.einsum(
        "qi,ei->qe", query_grad, query_weight, preferred_element_type=jnp.float32
    )
    memory_part = jnp.einsum("ki,ei->ke", key_grad, key_weight, preferred_element_type=jnp.float32)
    memory_part = memory_part + jnp.einsum(
        "ki,ei->ke", value_grad, value_weight, preferred_element_type=jnp.float32
    )
    return (decoder_part, memory_part)


def body(
    grad_in, memory, enc_grad_in, act_stash, slot_order, lengths, w_query, w_key, w_value, w_out
):
    held = memory[0]
    stash_local = act_stash[0]
    order_row = slot_order[0]
    length_row = lengths[0]
    head_count = lax.axis_size("head")
    shard_width = enc_grad_in.shape[2]
    feature_share = grad_in.shape[2] // head_count
    gradient = lax.dynamic_slice_in_dim(
        grad_in[0], lax.axis_index("head") * feature_share, feature_share, 1
    )
    carried = jnp.zeros((held.shape[0], shard_width * head_count), jnp.float32)
    carried = lax.dynamic_update_slice_in_dim(
        carried, enc_grad_in[0], lax.axis_index("head") * shard_width, 1
    )
    for tick_index in range(TICKS):
        if tick_index == 0:
            gradient_low = grad_in[0].astype(jnp.bfloat16)
        else:
            gradient_low = gathered_copies(gradient.astype(jnp.bfloat16), "head", 1)
        decoded = lax.dynamic_index_in_dim(stash_local, order_row[tick_index], 0, keepdims=False)
        decoder_part, memory_part = local_terms(
            gradient_low,
            held,
            decoded,
            length_row[tick_index],
            w_query[0],
            w_key[0],
            w_value[0],
            w_out[0],
        )
        gradient = gradient + sent_and_summed(decoder_part, "head", 1)
        carried = carried + memory_part
        gradient, carried = shifted((gradient, carried), "segment", -1)
        if tick_index + 1 < TICKS:
            held = shifted(held, "segment", -1)
    carried = sent_and_summed(carried, "head", 1)
    gradient = gathered_copies(gradient, "head", 1)
    return (gradient[None], carried[None])


def solution(mesh):
    in_specs = (
        P("segment", None, None),
        P("segment", None, None),
        P("segment", None, "head"),
        P("segment", None, None, None),
        P("segment", None),
        P("segment", None),
        P("segment", None, "head"),
        P("segment", None, "head"),
        P("segment", None, "head"),
        P("segment", "head", None),
    )
    out_specs = (P("segment", None, None), P("segment", None, "head"))
    return jax.shard_map(body, mesh=mesh, in_specs=in_specs, out_specs=out_specs, check_vma=False)
```

profile of v0, /device:TPU:1, one launch (start us, length us, event | category | flops | bytes accessed | tf_op | source)
XLA Modules:
  0.0 236.2 jit_solution(11993997918114420040)
XLA Ops:
  0.7 11.9 %collective-permute-start.1 = (bf16[128,512]{1,0:T(8,128)(2,1)}, bf16[128,512]{1,0:T(8,128)(2,1)}, u32[]{:S(2)}, u32[]{:S(2)}) collective-permute-start(bf16[128,512]{1,0:T(8,128)(2,1)} %bitcast.228), channel_id=1, source_target_pairs={{0,760},{8,0},{16,8},{24,16},{32,24},{40,32},{48,40},{56,48},{64,5... | collective-permute-start | bytes 393224 | tf_op jit(solution)/shard_map/ppermute | solution.py:42
  14.5 1.4 fusion.59
  18.6 2.2 convolution_convert_fusion.18
  20.8 1.8 copy.137
  23.7 1.8 copy.135
  26.5 2.1 fusion.61
  28.5 1.5 multiply_reduce_fusion.2
  32.4 14.3 %all-to-all-start = ((f32[8,128,64]{1,2,0:T(8,128)}), f32[8,128,64]{1,2,0:T(8,128)}, u32[]{:S(2)}, u32[]{:S(2)}) async-start(f32[8,128,64]{1,2,0:T(8,128)} %convolution_bitcast_fusion.2), calls=%async_computation | async-start | bytes 524288 | tf_op jit(solution)/shard_map/all_to_all | solution.py:35
  46.6 2.4 %convolution_convert_fusion.4 = bf16[8,128,128]{2,1,0:T(8,128)(2,1)} fusion(bf16[128,8,128]{0,2,1:T(8,128)(2,1)} %bitcast.234, f32[8,128]{1,0:T(8,128)S(1)} %get-tuple-element.12, bf16[128,8,128]{0,2,1:T(8,128)(2,1)} %bitcast.214, bf16[128,8,128]{0,2,1:T(8,128)(2,1)} %bitcast.217, pred[128]{0:T(512)(128)(4,1)S(1)} %iota_compare_fusion.2), kind=kOutput, calls=%fused_computation.16 | convolution fusion | flops 67765376 | bytes 1052800 | tf_op jit(solution)/shard_map/hqk,qhd->khd/dot_general | solution.py:88
  49.0 1.9 convolution_convert_fusion.5
  51.0 1.4 fusion.29
  52.5 1.4 convolution_add_fusion.2
  54.7 1.7 add.53
  56.5 1.9 collective-permute-start.5
  65.4 1.9 convolution_convert_fusion.14
  70.8 1.9 collective-permute-start
  72.8 1.9 convolution_convert_fusion.15
  74.7 1.8 copy.138
  76.5 1.9 collective-permute-start.3
  79.1 11.4 %all-to-all-start.1 = ((bf16[8,128,64]{1,2,0:T(8,128)(2,1)}), bf16[8,128,64]{1,2,0:T(8,128)(2,1)S(1)}, u32[]{:S(2)}, u32[]{:S(2)}) async-start(bf16[8,128,64]{1,2,0:T(8,128)(2,1)} %broadcast_in_dim.58), calls=%async_computation.1 | async-start | bytes 262144 | tf_op jit(solution)/shard_map/all_to_all | solution.py:12
  90.4 1.9 fusion.10
  92.4 2.1 fusion.62
  94.5 6.1 %all-to-all-done.1 = bf16[8,128,64]{1,2,0:T(8,128)(2,1)S(1)} async-done(((bf16[8,128,64]{1,2,0:T(8,128)(2,1)}), bf16[8,128,64]{1,2,0:T(8,128)(2,1)S(1)}, u32[]{:S(2)}, u32[]{:S(2)}) %all-to-all-start.1) | async-done | bytes 131104 | tf_op jit(solution)/shard_map/all_to_all | solution.py:12
  100.6 1.7 convolution_convert_fusion.13
  103.1 1.5 multiply_reduce_fusion.1
  107.0 4.8 %all-to-all-start.2 = ((f32[8,128,64]{1,2,0:T(8,128)}), f32[8,128,64]{1,2,0:T(8,128)}, u32[]{:S(2)}, u32[]{:S(2)}) async-start(f32[8,128,64]{1,2,0:T(8,128)} %convolution_bitcast_fusion.1), calls=%async_computation.2 | async-start | bytes 524288 | tf_op jit(solution)/shard_map/all_to_all | solution.py:35
  111.7 1.9 convolution_convert_fusion.10
  113.7 1.8 copy.141
  115.4 1.9 fusion.11
  117.4 2.2 fusion.63
  119.5 1.9 convolution_convert_fusion.3
  121.5 3.9 %all-to-all-done.2 = f32[8,128,64]{1,2,0:T(8,128)} async-done(((f32[8,128,64]{1,2,0:T(8,128)}), f32[8,128,64]{1,2,0:T(8,128)}, u32[]{:S(2)}, u32[]{:S(2)}) %all-to-all-start.2) | async-done | bytes 262176 | tf_op jit(solution)/shard_map/all_to_all | solution.py:35
  126.4 9.3 %collective-permute-start.2 = (f32[128,64]{0,1:T(8,128)S(1)}, f32[128,64]{0,1:T(8,128)S(1)}, u32[]{:S(2)}, u32[]{:S(2)}) collective-permute-start(f32[128,64]{0,1:T(8,128)S(1)} %add.48), channel_id=1, source_target_pairs={{0,760},{8,0},{16,8},{24,16},{32,24},{40,32},{48,40},{56,48},{64,5... | collective-permute-start | bytes 98312 | tf_op jit(solution)/shard_map/ppermute | solution.py:42
  138.2 5.6 %all-to-all-start.3 = ((bf16[8,128,64]{1,2,0:T(8,128)(2,1)}), bf16[8,128,64]{1,2,0:T(8,128)(2,1)S(1)}, u32[]{:S(2)}, u32[]{:S(2)}) async-start(bf16[8,128,64]{1,2,0:T(8,128)(2,1)} %broadcast_in_dim.60), calls=%async_computation.3 | async-start | bytes 262144 | tf_op jit(solution)/shard_map/all_to_all | solution.py:12
  143.8 2.3 convolution_convert_fusion.2
  146.0 2.3 fusion.12
  148.3 9.1 %collective-permute-start.6 = (f32[128,512]{1,0:T(8,128)}, f32[128,512]{1,0:T(8,128)}, u32[]{:S(2)}, u32[]{:S(2)}) collective-permute-start(f32[128,512]{1,0:T(8,128)} %fusion.12), channel_id=1, source_target_pairs={{0,760},{8,0},{16,8},{24,16},{32,24},{40,32},{48,40},{56,48},{64,5... | collective-permute-start | bytes 786440 | tf_op jit(solution)/shard_map/ppermute | solution.py:42
  157.4 1.7 convolution_convert_fusion.8
  160.0 1.5 multiply_reduce_fusion
  165.9 11.2 %all-to-all-start.4 = ((f32[8,128,64]{1,2,0:T(8,128)}), f32[8,128,64]{1,2,0:T(8,128)S(1)}, u32[]{:S(2)}, u32[]{:S(2)}) async-start(f32[8,128,64]{1,2,0:T(8,128)} %convolution_bitcast_fusion), calls=%async_computation.4 | async-start | bytes 524288 | tf_op jit(solution)/shard_map/all_to_all | solution.py:35
  177.1 1.6 convolution_convert_fusion
  180.2 1.9 collective-permute-start.7
  182.1 8.4 %collective-permute-done.7 = f32[128,512]{1,0:T(8,128)S(1)} collective-permute-done((f32[128,512]{1,0:T(8,128)S(1)}, f32[128,512]{1,0:T(8,128)S(1)}, u32[]{:S(2)}, u32[]{:S(2)}) %collective-permute-start.7) | collective-permute-done | bytes 262176 | tf_op jit(solution)/shard_map/ppermute | solution.py:42
  191.4 9.5 %all-to-all-start.6 = ((f32[8,128,64]{1,2,0:T(8,128)}), f32[8,128,64]{1,2,0:T(8,128)S(1)}, u32[]{:S(2)}, u32[]{:S(2)}) async-start(f32[8,128,64]{1,2,0:T(8,128)} %bitcast.49), calls=%async_computation.6 | async-start | bytes 524288 | tf_op jit(solution)/shard_map/all_to_all | solution.py:35
  201.7 7.0 %collective-permute-start.4 = (f32[128,64]{0,1:T(8,128)S(1)}, f32[128,64]{0,1:T(8,128)S(1)}, u32[]{:S(2)}, u32[]{:S(2)}) collective-permute-start(f32[128,64]{0,1:T(8,128)S(1)} %add.50), channel_id=1, source_target_pairs={{0,760},{8,0},{16,8},{24,16},{32,24},{40,32},{48,40},{56,48},{64,5... | collective-permute-start | bytes 98312 | tf_op jit(solution)/shard_map/ppermute | solution.py:42
  209.7 3.1 %all-to-all-done.6 = f32[8,128,64]{1,2,0:T(8,128)S(1)} async-done(((f32[8,128,64]{1,2,0:T(8,128)}), f32[8,128,64]{1,2,0:T(8,128)S(1)}, u32[]{:S(2)}, u32[]{:S(2)}) %all-to-all-start.6) | async-done | bytes 262176 | tf_op jit(solution)/shard_map/all_to_all | solution.py:35
  213.5 8.6 %all-to-all-start.5 = ((f32[8,128,64]{1,2,0:T(8,128)}), f32[8,128,64]{1,2,0:T(8,128)S(1)}, u32[]{:S(2)}, u32[]{:S(2)}) async-start(f32[8,128,64]{1,2,0:T(8,128)} %broadcast_in_dim.61), calls=%async_computation.5 | async-start | bytes 524288 | tf_op jit(solution)/shard_map/all_to_all | solution.py:12
  222.7 12.6 %all-to-all-done.5 = f32[8,128,64]{1,2,0:T(8,128)S(1)} async-done(((f32[8,128,64]{1,2,0:T(8,128)}), f32[8,128,64]{1,2,0:T(8,128)S(1)}, u32[]{:S(2)}, u32[]{:S(2)}) %all-to-all-start.5) | async-done | bytes 262176 | tf_op jit(solution)/shard_map/all_to_all | solution.py:12
  (105 shorter events, 33.2 us)
Async XLA Ops:
  0.6 16.5 %copy-start = (bf16[1,512,1024]{2,1,0:T(8,128)(2,1)S(1)}, bf16[1,512,1024]{2,1,0:T(8,128)(2,1)}, u32[]{:S(2)}) copy-start(bf16[1,512,1024]{2,1,0:T(8,128)(2,1)} %param.16) | copy-start | bytes 3145732
  0.6 11.9 %copy-start.24 = (s32[1,3]{1,0:T(1,128)S(1)}, s32[1,3]{1,0:T(1,128)}, u32[]{:S(2)}) copy-start(s32[1,3]{1,0:T(1,128)} %param.14) | copy-start | bytes 40
  0.7 17.9 %copy-start.3 = (bf16[1,1024,512]{2,1,0:T(8,128)(2,1)S(1)}, bf16[1,1024,512]{2,1,0:T(8,128)(2,1)}, u32[]{:S(2)}) copy-start(bf16[1,1024,512]{2,1,0:T(8,128)(2,1)} %param.19) | copy-start | bytes 3145732
  0.7 72.1 %collective-permute-start.1 = (bf16[128,512]{1,0:T(8,128)(2,1)}, bf16[128,512]{1,0:T(8,128)(2,1)}, u32[]{:S(2)}, u32[]{:S(2)}) collective-permute-start(bf16[128,512]{1,0:T(8,128)(2,1)} %bitcast.228), channel_id=1, source_target_pairs={{0,760},{8,0},{16,8},{24,16},{32,24},{40,32},{48,40},{56,48},{64,5... | collective-permute-start | bytes 393224 | tf_op jit(solution)/shard_map/ppermute | solution.py:42
  18.6 7.9 %copy-start.10 = (bf16[128,1024]{0,1:T(8,128)(2,1)}, bf16[128,1024]{0,1:T(8,128)(2,1)S(1)}, u32[]{:S(2)}) copy-start(bf16[128,1024]{0,1:T(8,128)(2,1)S(1)} %copy.136) | copy-start | bytes 786436
  18.6 4.1 %copy-start.1 = (bf16[1,512,1024]{2,1,0:T(8,128)(2,1)S(1)}, bf16[1,512,1024]{2,1,0:T(8,128)(2,1)}, u32[]{:S(2)}) copy-start(bf16[1,512,1024]{2,1,0:T(8,128)(2,1)} %param.17) | copy-start | bytes 3145732
  20.8 1.8 copy-start.17
  22.6 2.8 %copy-start.2 = (bf16[1,512,1024]{2,1,0:T(8,128)(2,1)S(1)}, bf16[1,512,1024]{2,1,0:T(8,128)(2,1)}, u32[]{:S(2)}) copy-start(bf16[1,512,1024]{2,1,0:T(8,128)(2,1)} %param.18) | copy-start | bytes 3145732
  28.5 1.5 copy-start.16
  30.0 1.0 copy-start.11
  32.4 37.4 %all-to-all-start = ((f32[8,128,64]{1,2,0:T(8,128)}), f32[8,128,64]{1,2,0:T(8,128)}, u32[]{:S(2)}, u32[]{:S(2)}) async-start(f32[8,128,64]{1,2,0:T(8,128)} %convolution_bitcast_fusion.2), calls=%async_computation | async-start | bytes 524288 | tf_op jit(solution)/shard_map/all_to_all | solution.py:35
  49.0 2.0 copy-start.23
  53.9 0.7 copy-start.18
  56.5 89.6 %collective-permute-start.5 = (f32[128,512]{1,0:T(8,128)}, f32[128,512]{1,0:T(8,128)}, u32[]{:S(2)}, u32[]{:S(2)}) collective-permute-start(f32[128,512]{1,0:T(8,128)} %add.53), channel_id=1, source_target_pairs={{0,760},{8,0},{16,8},{24,16},{32,24},{40,32},{48,40},{56,48},{64,5... | collective-permute-start | bytes 786440 | tf_op jit(solution)/shard_map/ppermute | solution.py:42
  68.5 23.9 %copy-start.5 = (bf16[128,1024]{0,1:T(8,128)(2,1)}, bf16[128,1024]{0,1:T(8,128)(2,1)S(1)}, u32[]{:S(2)}) copy-start(bf16[128,1024]{0,1:T(8,128)(2,1)S(1)} %copy.139) | copy-start | bytes 786436
  70.8 7.6 %collective-permute-start = (f32[128,64]{0,1:T(8,128)S(1)}, f32[128,64]{0,1:T(8,128)S(1)}, u32[]{:S(2)}, u32[]{:S(2)}) collective-permute-start(f32[128,64]{0,1:T(8,128)S(1)} %bitcast_add_fusion.1), channel_id=1, source_target_pairs={{0,760},{8,0},{16,8},{24,16},{32,24},{40,32},{48,40},{56,48},{64,5... | collective-permute-start | bytes 98312 | tf_op jit(solution)/shard_map/ppermute | solution.py:42
  76.5 35.3 %collective-permute-start.3 = (bf16[128,512]{1,0:T(8,128)(2,1)}, bf16[128,512]{1,0:T(8,128)(2,1)}, u32[]{:S(2)}, u32[]{:S(2)}) collective-permute-start(bf16[128,512]{1,0:T(8,128)(2,1)} %collective-permute-done.1), channel_id=1, source_target_pairs={{0,760},{8,0},{16,8},{24,16},{32,24},{40,32},{48,40},{56,48},{64,5... | collective-permute-start | bytes 393224 | tf_op jit(solution)/shard_map/ppermute | solution.py:42
  78.4 0.7 copy-start.21
  79.1 21.5 %all-to-all-start.1 = ((bf16[8,128,64]{1,2,0:T(8,128)(2,1)}), bf16[8,128,64]{1,2,0:T(8,128)(2,1)S(1)}, u32[]{:S(2)}, u32[]{:S(2)}) async-start(bf16[8,128,64]{1,2,0:T(8,128)(2,1)} %broadcast_in_dim.58), calls=%async_computation.1 | async-start | bytes 262144 | tf_op jit(solution)/shard_map/all_to_all | solution.py:12
  103.1 1.5 copy-start.15
  104.6 1.0 copy-start.7
  107.0 18.4 %all-to-all-start.2 = ((f32[8,128,64]{1,2,0:T(8,128)}), f32[8,128,64]{1,2,0:T(8,128)}, u32[]{:S(2)}, u32[]{:S(2)}) async-start(f32[8,128,64]{1,2,0:T(8,128)} %convolution_bitcast_fusion.1), calls=%async_computation.2 | async-start | bytes 524288 | tf_op jit(solution)/shard_map/all_to_all | solution.py:35
  121.5 4.9 %copy-start.22 = (f32[128,64]{0,1:T(8,128)S(1)}, f32[128,64]{0,1:T(8,128)}, u32[]{:S(2)}) copy-start(f32[128,64]{0,1:T(8,128)} %copy-done.21) | copy-start | bytes 98308
  121.5 14.2 %copy-start.12 = (bf16[8,128,128]{2,1,0:T(8,128)(2,1)S(1)}, bf16[8,128,128]{2,1,0:T(8,128)(2,1)}, u32[]{:S(2)}) copy-start(bf16[8,128,128]{2,1,0:T(8,128)(2,1)} %convolution_convert_fusion.3) | copy-start | bytes 786436
  126.4 10.5 %collective-permute-start.2 = (f32[128,64]{0,1:T(8,128)S(1)}, f32[128,64]{0,1:T(8,128)S(1)}, u32[]{:S(2)}, u32[]{:S(2)}) collective-permute-start(f32[128,64]{0,1:T(8,128)S(1)} %add.48), channel_id=1, source_target_pairs={{0,760},{8,0},{16,8},{24,16},{32,24},{40,32},{48,40},{56,48},{64,5... | collective-permute-start | bytes 98312 | tf_op jit(solution)/shard_map/ppermute | solution.py:42
  136.9 6.9 %copy-start.6 = (bf16[128,1024]{0,1:T(8,128)(2,1)S(1)}, bf16[128,1024]{0,1:T(8,128)(2,1)}, u32[]{:S(2)}) copy-start(bf16[128,1024]{0,1:T(8,128)(2,1)} %copy-done.5) | copy-start | bytes 786436
  136.9 0.6 copy-start.19
  138.2 19.2 %all-to-all-start.3 = ((bf16[8,128,64]{1,2,0:T(8,128)(2,1)}), bf16[8,128,64]{1,2,0:T(8,128)(2,1)S(1)}, u32[]{:S(2)}, u32[]{:S(2)}) async-start(bf16[8,128,64]{1,2,0:T(8,128)(2,1)} %broadcast_in_dim.60), calls=%async_computation.3 | async-start | bytes 262144 | tf_op jit(solution)/shard_map/all_to_all | solution.py:12
  148.3 30.9 %collective-permute-start.6 = (f32[128,512]{1,0:T(8,128)}, f32[128,512]{1,0:T(8,128)}, u32[]{:S(2)}, u32[]{:S(2)}) collective-permute-start(f32[128,512]{1,0:T(8,128)} %fusion.12), channel_id=1, source_target_pairs={{0,760},{8,0},{16,8},{24,16},{32,24},{40,32},{48,40},{56,48},{64,5... | collective-permute-start | bytes 786440 | tf_op jit(solution)/shard_map/ppermute | solution.py:42
  160.0 1.5 copy-start.14
  161.5 1.0 copy-start.4
  162.4 0.9 copy-start.8
  165.9 11.2 %copy-start.9 = (bf16[128,1024]{0,1:T(8,128)(2,1)S(1)}, bf16[128,1024]{0,1:T(8,128)(2,1)}, u32[]{:S(2)}) copy-start(bf16[128,1024]{0,1:T(8,128)(2,1)} %copy.141) | copy-start | bytes 786436
  165.9 25.5 %all-to-all-start.4 = ((f32[8,128,64]{1,2,0:T(8,128)}), f32[8,128,64]{1,2,0:T(8,128)S(1)}, u32[]{:S(2)}, u32[]{:S(2)}) async-start(f32[8,128,64]{1,2,0:T(8,128)} %convolution_bitcast_fusion), calls=%async_computation.4 | async-start | bytes 524288 | tf_op jit(solution)/shard_map/all_to_all | solution.py:35
  177.1 1.6 copy-start.13
  180.2 10.3 %collective-permute-start.7 = (f32[128,512]{1,0:T(8,128)S(1)}, f32[128,512]{1,0:T(8,128)S(1)}, u32[]{:S(2)}, u32[]{:S(2)}) collective-permute-start(f32[128,512]{1,0:T(8,128)S(1)} %add.57), channel_id=1, source_target_pairs={{0,760},{8,0},{16,8},{24,16},{32,24},{40,32},{48,40},{56,48},{64,5... | collective-permute-start | bytes 786440 | tf_op jit(solution)/shard_map/ppermute | solution.py:42
  191.4 21.4 %all-to-all-start.6 = ((f32[8,128,64]{1,2,0:T(8,128)}), f32[8,128,64]{1,2,0:T(8,128)S(1)}, u32[]{:S(2)}, u32[]{:S(2)}) async-start(f32[8,128,64]{1,2,0:T(8,128)} %bitcast.49), calls=%async_computation.6 | async-start | bytes 524288 | tf_op jit(solution)/shard_map/all_to_all | solution.py:35
  200.9 0.8 copy-start.20
  201.7 8.0 %collective-permute-start.4 = (f32[128,64]{0,1:T(8,128)S(1)}, f32[128,64]{0,1:T(8,128)S(1)}, u32[]{:S(2)}, u32[]{:S(2)}) collective-permute-start(f32[128,64]{0,1:T(8,128)S(1)} %add.50), channel_id=1, source_target_pairs={{0,760},{8,0},{16,8},{24,16},{32,24},{40,32},{48,40},{56,48},{64,5... | collective-permute-start | bytes 98312 | tf_op jit(solution)/shard_map/ppermute | solution.py:42
  213.5 21.8 %all-to-all-start.5 = ((f32[8,128,64]{1,2,0:T(8,128)}), f32[8,128,64]{1,2,0:T(8,128)S(1)}, u32[]{:S(2)}, u32[]{:S(2)}) async-start(f32[8,128,64]{1,2,0:T(8,128)} %broadcast_in_dim.61), calls=%async_computation.5 | async-start | bytes 524288 | tf_op jit(solution)/shard_map/all_to_all | solution.py:12
where the time goes:
time: 238 us; the launch traced here: 236 us
  starting transfers between devices  110 us (46%)
  matrix products  53 us (22%)
  waiting for transfers between devices  35.1 us (15%)
  local copies, waits for them, and re-layouts  24.9 us (10%)
  between operations  7.08 us (3%)
  other arithmetic  5.8 us (2%)
    ppermute x8, starting transfers between devices, shifted(): return lax.ppermute(value, axis, pairs)  45 us
    all_to_all x4, starting transfers between devices, sent_and_summed(): lax.all_to_all(pieces, axis, split_axis=0, concat_axis=0, tiled=True)  39.8 us
    all_to_all x3, starting transfers between devices, copy_for_each(): lax.all_to_all(jnp.broadcast_to(shard[None], (length, *shard.shape)), axi...  25.5 us
    all_to_all x3, waiting for transfers between devices, copy_for_each(): lax.all_to_all(jnp.broadcast_to(shard[None], (length, *shard.shape)), axi...  18.7 us
    ppermute x8, waiting for transfers between devices, shifted(): return lax.ppermute(value, axis, pairs)  9.44 us
    all_to_all x4, waiting for transfers between devices, sent_and_summed(): lax.all_to_all(pieces, axis, split_axis=0, concat_axis=0, tiled=True)  7 us
    unnamed x53, local copies, waits for them, and re-layouts  6.35 us
    sub x3, matrix products, local_terms(): expo = jnp.exp(scores - row_max)  6.35 us
  transfers between devices with their start and end apart: 15, of which 6 were waited for; matrix products, arithmetic and copies ran while one was open for 33% of the time, Pallas kernels for 0%

commit v1 on v0

v1 whole, which is shorter than its diff:
```python
import jax
import jax.numpy as jnp
from jax import lax
from jax.experimental import pallas as pl
from jax.experimental.pallas import tpu as pltpu
from jax.sharding import PartitionSpec as P

HEAD_DIM = 128
TICKS = 3
MESH = pl.DeviceIdType.MESH
F32 = jnp.float32
BF16 = jnp.bfloat16
ORDER = (0, 2, 1, 3)


def nn(a, b):
    return lax.dot_general(a, b, (((1,), (0,)), ((), ())), preferred_element_type=F32)


def nt(a, b):
    return lax.dot_general(a, b, (((1,), (1,)), ((), ())), preferred_element_type=F32)


def tn(a, b):
    return lax.dot_general(a, b, (((0,), (0,)), ((), ())), preferred_element_type=F32)


def kernel(
    grad_hbm, mem_hbm, enc_hbm, stash_hbm, slot_ref, len_ref, wq_hbm, wk_hbm, wv_hbm, wo_hbm,
    gout_ref, eout_ref,
    grad_v, stash_v, wq, wk, wv, wo, held, q_s, k_s, v_s, att, cg_s, sg_s, qg_s, kg_s, vg_s,
    gl, gres, dpf, dpb, sibr, r1s, r1r, r2s, r2x, r2y, gfin,
    mpf, mpb, mpr, cs, cr, fin, esw, esr, encr,
    load_sem, sib_s, sib_r, r1_ss, r1_rs, x_ss, x_rs, y_ss, y_rs, fw_ss, fw_rs,
    mp_ss, mp_rs, c_ss, c_rs, f_ss, f_rs, h_ss, h_rs, hf_ss, hf_rs, e_ss, e_rs, w_ss, w_rs,
):
    heads = wq.shape[1] // HEAD_DIM
    seg = lax.axis_index("segment")
    head = lax.axis_index("head")
    segments = lax.axis_size("segment")
    c = head // 2
    k = head % 2
    prev = (seg + segments - 1) % segments
    prev3 = (seg + 3 * segments - 3) % segments
    nxt = (seg + 1) % segments
    nxt3 = (seg + 3) % segments
    c1 = c + 1 - 2 * (c % 2)
    c3 = 3 - c
    sib = (seg, 2 * c + 1 - k)
    mine = pl.ds(pl.multiple_of(64 * k, 64), 64)
    other = pl.ds(pl.multiple_of(64 * (1 - k), 64), 64)

    def rcopy(src, dst, ss, rs, dev):
        return pltpu.make_async_remote_copy(
            src_ref=src, dst_ref=dst, send_sem=ss, recv_sem=rs, device_id=dev, device_id_type=MESH
        )

    sends = []

    def go(copy):
        copy.start()
        sends.append(copy)
        return copy

    loads = {}

    def load(name, src, dst):
        copy = pltpu.make_async_copy(src, dst, load_sem.at[len(loads)])
        copy.start()
        loads[name] = copy

    load("mem", mem_hbm.at[0], held.at[0])
    load("wk", wk_hbm.at[0], wk)
    load("stash", stash_hbm.at[0], stash_v)
    load("wq", wq_hbm.at[0], wq)
    load("wv", wv_hbm.at[0], wv)
    load("grad", grad_hbm.at[0], grad_v)
    load("wo", wo_hbm.at[0], wo)

    barrier = pltpu.get_barrier_semaphore()
    senders = [sib, (seg, 2 * c1 + k), (seg, 2 * c3 + k), (nxt3, head)]
    senders += [(nxt, 2 * ((c + r) % 4) + k) for r in range(4)]
    for dev in senders:
        pl.semaphore_signal(barrier, inc=1, device_id=dev, device_id_type=MESH)

    def keys_of(t):
        k_s[...] = jnp.concatenate(
            [nn(held[t], wk[:, 256 * n : 256 * n + 256]).astype(BF16) for n in range(4)], axis=1
        )

    def values_of(t):
        v_s[...] = jnp.concatenate(
            [nn(held[t], wv[:, 256 * n : 256 * n + 256]).astype(BF16) for n in range(4)], axis=1
        )

    def queries_of(t):
        decoded = stash_v[slot_ref[0, t]]
        q_s[...] = jnp.concatenate(
            [nn(decoded, wq[:, 256 * n : 256 * n + 256]).astype(BF16) for n in range(4)], axis=1
        )

    def softmax_of(t):
        allowed = lax.broadcasted_iota(jnp.int32, (128, 128), 1) < len_ref[0, t]
        for h in range(heads):
            at = slice(HEAD_DIM * h, HEAD_DIM * h + HEAD_DIM)
            scores = jnp.where(allowed, nt(q_s[:, at], k_s[:, at]), F32(-1e30))
            expo = jnp.exp(scores - jnp.max(scores, axis=-1, keepdims=True))
            att[h] = expo / jnp.sum(expo, axis=-1, keepdims=True)

    loads["mem"].wait()
    loads["wk"].wait()
    keys_of(0)
    loads["stash"].wait()
    loads["wq"].wait()
    queries_of(0)

    pl.semaphore_wait(barrier, 8)
    helds = [
        rcopy(held.at[t, mine], held.at[t + 1, mine], h_ss.at[t], h_rs.at[t], (prev, head))
        for t in range(TICKS - 1)
    ]
    held_fw = [
        rcopy(held.at[t + 1, mine], held.at[t + 1, mine], hf_ss.at[t], hf_rs.at[t], sib)
        for t in range(TICKS - 1)
    ]
    go(helds[0])
    enc_copy = go(rcopy(enc_hbm.at[0], encr, e_ss, e_rs, (prev3, head)))

    softmax_of(0)
    loads["wv"].wait()
    values_of(0)
    loads["grad"].wait()
    for j in range(4):
        cols = slice(128 * j, 128 * j + 128)
        gl[0, j] = grad_v[:, cols].astype(BF16)
        gres[j] = grad_v[mine, cols]
    loads["wo"].wait()

    for t in range(TICKS):
        last = t == TICKS - 1
        g = jnp.concatenate([gl[t, j] for j in range(4)], axis=1)
        for n in range(4):
            cg_s[:, 256 * n : 256 * n + 256] = nt(g, wo[256 * n : 256 * n + 256, :]).astype(BF16)
        for h in range(heads):
            at = slice(HEAD_DIM * h, HEAD_DIM * h + HEAD_DIM)
            prob_grad = nt(cg_s[:, at], v_s[:, at])
            weight = att[h]
            total = jnp.sum(weight * prob_grad, axis=-1, keepdims=True)
            score_grad = (weight * (prob_grad - total)).astype(BF16)
            sg_s[h] = score_grad
            qg_s[:, at] = nn(score_grad, k_s[:, at]).astype(BF16)
        pair = {}
        for j in ORDER:
            part = nt(qg_s[...], wq[128 * j : 128 * j + 128, :])
            dpf[j] = part
            dpb[t, j] = part.astype(BF16)
            pair[j] = go(
                rcopy(dpb.at[t, j, other], sibr.at[t, j], sib_s.at[t, j], sib_r.at[t, j], sib)
            )
        first = {}
        for j in ORDER:
            pair[j].wait_recv()
            r1s[t, j] = (dpf[j, mine] + sibr[t, j].astype(F32)).astype(BF16)
            partner = c1 if j < 2 else c3
            first[j] = go(
                rcopy(
                    r1s.at[t, j], r1r.at[t, j], r1_ss.at[t, j], r1_rs.at[t, j],
                    (seg, 2 * partner + k),
                )
            )
        for h in range(heads):
            at = slice(HEAD_DIM * h, HEAD_DIM * h + HEAD_DIM)
            vg_s[:, at] = tn(att[h].astype(BF16), cg_s[:, at]).astype(BF16)
            kg_s[:, at] = tn(sg_s[h], q_s[:, at]).astype(BF16)
        for j in range(4):
            rows = slice(128 * j, 128 * j + 128)
            part = nt(kg_s[...], wk[rows, :]) + nt(vg_s[...], wv[rows, :])
            mpf[j] = part
            mpb[t, j] = part.astype(BF16)
        mp_copy = go(rcopy(mpb.at[t, :, other], mpr.at[t], mp_ss.at[t], mp_rs.at[t], sib))

        def carry():
            mp_copy.wait_recv()
            if t > 0:
                carried[t - 1].wait_recv()
            for j in range(4):
                part = mpf[j, mine] + mpr[t, j].astype(F32)
                if t > 0:
                    part = part + cr[t - 1, j].astype(F32)
                cs[t, j] = part.astype(BF16)

        if t == 0:
            carried = [
                rcopy(cs.at[i], cr.at[i], c_ss.at[i], c_rs.at[i], (prev, head))
                for i in range(TICKS - 1)
            ]
        if not last:
            helds[t].wait_recv()
            go(held_fw[t])
            if t + 1 < TICKS - 1:
                go(helds[t + 1])
            held_fw[t].wait_recv()
            keys_of(t + 1)
            values_of(t + 1)
        else:
            carry()
            final = []
            for r in range(4):
                dest = (c + r) % 4
                final.append(
                    go(rcopy(cs.at[t, dest], fin.at[r], f_ss.at[r], f_rs.at[r], (prev, 2 * dest + k)))
                )
        straight, across = {}, {}
        for j in ORDER:
            first[j].wait_recv()
            side = (c // 2) if j < 2 else ((c + 1) // 2) % 2
            keep = jnp.where(side == 0, F32(1.0), F32(0.0))
            total = r1s[t, j].astype(F32) + r1r[t, j].astype(F32) + keep * gres[j]
            r2s[t, j] = total.astype(BF16)
            partner = c3 if j < 2 else c1
            across[j] = go(
                rcopy(
                    r2s.at[t, j], r2y.at[t, j], y_ss.at[t, j], y_rs.at[t, j],
                    (prev, 2 * partner + k),
                )
            )
            straight[j] = go(
                rcopy(r2s.at[t, j], r2x.at[t, j], x_ss.at[t, j], x_rs.at[t, j], (prev, head))
            )
        if not last:
            carry()
            go(carried[t])
            queries_of(t + 1)
            softmax_of(t + 1)
        else:
            for r in range(4):
                final[r].wait_recv()
            total = fin[0].astype(F32) + fin[1].astype(F32) + fin[2].astype(F32) + fin[3].astype(F32)
            esw[...] = total
            swap = go(rcopy(esw, esr, w_ss, w_rs, sib))
        forward = {}
        for j in ORDER:
            straight[j].wait_recv()
            across[j].wait_recv()
            total = r2x[t, j].astype(F32) + r2y[t, j].astype(F32)
            if last:
                gfin[j, mine] = total
                part = gfin.at[j, mine]
            else:
                gres[j] = total
                gl[t + 1, j, mine] = total.astype(BF16)
                part = gl.at[t + 1, j, mine]
            forward[j] = go(rcopy(part, part, fw_ss.at[t, j], fw_rs.at[t, j], sib))
        for j in ORDER:
            forward[j].wait_recv()

    for j in range(4):
        gout_ref[0, :, 128 * j : 128 * j + 128] = gfin[j]
    swap.wait_recv()
    enc_copy.wait_recv()

    def my_columns(x):
        return jnp.where(k == 0, x[:, :64], x[:, 64:])

    eout_ref[0, mine, :] = encr[mine, :] + my_columns(esw[...])
    eout_ref[0, other, :] = encr[other, :] + my_columns(esr[...])
    for copy in sends:
        copy.wait_send()


def body(
    grad_in, memory, enc_grad_in, act_stash, slot_order, lengths, w_query, w_key, w_value, w_out
):
    inner = w_query.shape[2]
    heads = inner // HEAD_DIM
    anywhere = pl.BlockSpec(memory_space=pl.ANY)
    scalars = pl.BlockSpec(memory_space=pltpu.SMEM)
    whole = pl.BlockSpec(memory_space=pltpu.VMEM)

    def dma(*shape):
        return pltpu.SemaphoreType.DMA(shape) if shape else pltpu.SemaphoreType.DMA

    V = pltpu.VMEM
    half = (64, 128)
    scratch = [
        V((128, 512), F32), V((TICKS, 128, 512), BF16),
        V((512, inner), BF16), V((512, inner), BF16), V((512, inner), BF16), V((inner, 512), BF16),
        V((TICKS, 128, 512), BF16),
        V((128, inner), BF16), V((128, inner), BF16), V((128, inner), BF16),
        V((heads, 128, 128), F32),
        V((128, inner), BF16), V((heads, 128, 128), BF16),
        V((128, inner), BF16), V((128, inner), BF16), V((128, inner), BF16),
        V((TICKS, 4, 128, 128), BF16), V((4, *half), F32),
        V((4, 128, 128), F32), V((TICKS, 4, 128, 128), BF16), V((TICKS, 4, *half), BF16),
        V((TICKS, 4, *half), BF16), V((TICKS, 4, *half), BF16),
        V((TICKS, 4, *half), BF16), V((TICKS, 4, *half), BF16), V((TICKS, 4, *half), BF16),
        V((4, 128, 128), F32),
        V((4, 128, 128), F32), V((TICKS, 4, 128, 128), BF16), V((TICKS, 4, *half), BF16),
        V((TICKS, 4, *half), BF16), V((TICKS - 1, 4, *half), BF16),
        V((4, *half), BF16), V(half, F32), V(half, F32), V((128, 64), F32),
        dma(7),
        dma(TICKS, 4), dma(TICKS, 4), dma(TICKS, 4), dma(TICKS, 4),
        dma(TICKS, 4), dma(TICKS, 4), dma(TICKS, 4), dma(TICKS, 4), dma(TICKS, 4), dma(TICKS, 4),
        dma(TICKS), dma(TICKS), dma(TICKS - 1), dma(TICKS - 1), dma(4), dma(4),
        dma(TICKS - 1), dma(TICKS - 1), dma(TICKS - 1), dma(TICKS - 1), dma(), dma(), dma(), dma(),
    ]
    return pl.pallas_call(
        kernel,
        name="relay_backward",
        out_shape=(
            jax.ShapeDtypeStruct(grad_in.shape, F32),
            jax.ShapeDtypeStruct(enc_grad_in.shape, F32),
        ),
        in_specs=[anywhere] * 4 + [scalars] * 2 + [anywhere] * 4,
        out_specs=(whole, whole),
        scratch_shapes=scratch,
        compiler_params=pltpu.CompilerParams(
            collective_id=0, has_side_effects=True, vmem_limit_bytes=40 * 1024 * 1024
        ),
        cost_estimate=pl.CostEstimate(
            flops=3_400_000_000, bytes_accessed=5_500_000, transcendentals=400_000
        ),
    )(grad_in, memory, enc_grad_in, act_stash, slot_order, lengths, w_query, w_key, w_value, w_out)


def solution(mesh):
    in_specs = (
        P("segment", None, None),
        P("segment", None, None),
        P("segment", None, "head"),
        P("segment", None, None, None),
        P("segment", None),
        P("segment", None),
        P("segment", None, "head"),
        P("segment", None, "head"),
        P("segment", None, "head"),
        P("segment", "head", None),
    )
    out_specs = (P("segment", None, None), P("segment", None, "head"))
    return jax.shard_map(body, mesh=mesh, in_specs=in_specs, out_specs=out_specs, check_vma=False)
```

time: 238 us -> 79 us (0.33)
  the two profiles are of different devices: /device:TPU:1 before, /device:TPU:59 now
where the time goes in v1:
time: 79 us; the launch traced here: 78.5 us
  Pallas kernels  67.8 us (86%)
  local copies, waits for them, and re-layouts  10 us (13%)
    pallas_call x1, Pallas kernels, body(): pl.pallas_call(kernel, name='relay_backward', out_shape=(jax.ShapeDtypeSt...  67.8 us
    unnamed x20, local copies, waits for them, and re-layouts  9.31 us

profile of v1, /device:TPU:59, one launch (start us, length us, event | category | flops | bytes accessed | tf_op | source)
XLA Modules:
  0.0 78.5 jit_solution(9894296082056604431)
XLA Ops:
  0.6 0.0 copy-start.8
  0.6 0.0 copy-start.7
  0.7 0.9 %copy.12.enc_hbm = f32[1,128,64]{2,1,0:T(8,128)S(1)} copy(f32[1,128,64]{1,2,0:T(8,128)} %param.12) | data formatting | bytes 65536 | tf_op args[2]
  1.5 0.0 copy-done.8
  1.5 0.0 copy-done.7
  1.5 0.0 copy-start
  1.5 1.2 %copy-done = bf16[1,512,1024]{2,1,0:T(8,128)(2,1)S(1)} copy-done((bf16[1,512,1024]{2,1,0:T(8,128)(2,1)S(1)}, bf16[1,512,1024]{2,1,0:T(8,128)(2,1)}, u32[]{:S(2)}) %copy-start) | copy-done | bytes 1048600
  2.8 0.0 copy-start.1
  2.8 1.2 %copy-done.1 = bf16[1,512,1024]{2,1,0:T(8,128)(2,1)S(1)} copy-done((bf16[1,512,1024]{2,1,0:T(8,128)(2,1)S(1)}, bf16[1,512,1024]{2,1,0:T(8,128)(2,1)}, u32[]{:S(2)}) %copy-start.1) | copy-done | bytes 1048600
  4.0 0.0 copy-start.2
  4.0 1.2 %copy-done.2 = bf16[1,512,1024]{2,1,0:T(8,128)(2,1)S(1)} copy-done((bf16[1,512,1024]{2,1,0:T(8,128)(2,1)S(1)}, bf16[1,512,1024]{2,1,0:T(8,128)(2,1)}, u32[]{:S(2)}) %copy-start.2) | copy-done | bytes 1048600
  5.2 0.0 copy-start.3
  5.2 1.2 %copy-done.3 = bf16[1,1024,512]{2,1,0:T(8,128)(2,1)S(1)} copy-done((bf16[1,1024,512]{2,1,0:T(8,128)(2,1)S(1)}, bf16[1,1024,512]{2,1,0:T(8,128)(2,1)}, u32[]{:S(2)}) %copy-start.3) | copy-done | bytes 1048600
  6.4 0.0 copy-start.4
  6.4 1.0 %copy-done.4 = bf16[1,3,128,512]{3,2,1,0:T(8,128)(2,1)S(1)} copy-done((bf16[1,3,128,512]{3,2,1,0:T(8,128)(2,1)S(1)}, bf16[1,3,128,512]{3,2,1,0:T(8,128)(2,1)}, u32[]{:S(2)}) %copy-start.4) | copy-done | bytes 393240
  7.4 0.0 copy-start.5
  7.4 0.9 %copy-done.5 = f32[1,128,512]{2,1,0:T(8,128)S(1)} copy-done((f32[1,128,512]{2,1,0:T(8,128)S(1)}, f32[1,128,512]{2,1,0:T(8,128)}, u32[]{:S(2)}) %copy-start.5) | copy-done | bytes 262168
  8.4 0.0 copy-start.6
  8.4 0.9 %copy-done.6 = bf16[1,128,512]{2,1,0:T(8,128)(2,1)S(1)} copy-done((bf16[1,128,512]{2,1,0:T(8,128)(2,1)S(1)}, bf16[1,128,512]{2,1,0:T(8,128)(2,1)}, u32[]{:S(2)}) %copy-start.6) | copy-done | bytes 131096
  9.3 67.8 %relay_backward.1 = (f32[1,128,512]{2,1,0:T(8,128)S(1)}, f32[1,128,64]{2,1,0:T(8,128)S(1)}) custom-call(f32[1,128,512]{2,1,0:T(8,128)S(1)} %copy-done.5, bf16[1,128,512]{2,1,0:T(8,128)(2,1)S(1)} %copy-done.6, f32[1,128,64]{2,1,0:T(8,128)S(1)} %copy.12.enc_hbm, bf16[1,3,128,512]{3,2,1,0:T(8,128)(2,1)S(1)} %copy-done.4, s32[1,3]{1,0:T(1,128)S(1)} %copy-done.7, ...), custom_call_target="tpu_custom_call" | custom-call | flops 3400000000 | bytes 5500000 | tf_op jit(solution)/shard_map/relay_backward/pallas_call | solution.py:307
  77.1 0.7 copy.13
  77.8 0.7 copy.15
Async XLA Ops:
  0.6 0.9 %copy-start.8 = (s32[1,3]{1,0:T(1,128)S(1)}, s32[1,3]{1,0:T(1,128)}, u32[]{:S(2)}) copy-start(s32[1,3]{1,0:T(1,128)} %len_ref.1) | copy-start | bytes 40
  0.6 0.9 %copy-start.7 = (s32[1,3]{1,0:T(1,128)S(1)}, s32[1,3]{1,0:T(1,128)}, u32[]{:S(2)}) copy-start(s32[1,3]{1,0:T(1,128)} %slot_ref.1) | copy-start | bytes 40
  1.5 1.2 %copy-start = (bf16[1,512,1024]{2,1,0:T(8,128)(2,1)S(1)}, bf16[1,512,1024]{2,1,0:T(8,128)(2,1)}, u32[]{:S(2)}) copy-start(bf16[1,512,1024]{2,1,0:T(8,128)(2,1)} %wq_hbm.1) | copy-start | bytes 3145732
  2.8 1.2 %copy-start.1 = (bf16[1,512,1024]{2,1,0:T(8,128)(2,1)S(1)}, bf16[1,512,1024]{2,1,0:T(8,128)(2,1)}, u32[]{:S(2)}) copy-start(bf16[1,512,1024]{2,1,0:T(8,128)(2,1)} %wk_hbm.1) | copy-start | bytes 3145732
  4.0 1.2 %copy-start.2 = (bf16[1,512,1024]{2,1,0:T(8,128)(2,1)S(1)}, bf16[1,512,1024]{2,1,0:T(8,128)(2,1)}, u32[]{:S(2)}) copy-start(bf16[1,512,1024]{2,1,0:T(8,128)(2,1)} %wv_hbm.1) | copy-start | bytes 3145732
  5.2 1.2 %copy-start.3 = (bf16[1,1024,512]{2,1,0:T(8,128)(2,1)S(1)}, bf16[1,1024,512]{2,1,0:T(8,128)(2,1)}, u32[]{:S(2)}) copy-start(bf16[1,1024,512]{2,1,0:T(8,128)(2,1)} %wo_hbm.1) | copy-start | bytes 3145732
  6.4 1.0 %copy-start.4 = (bf16[1,3,128,512]{3,2,1,0:T(8,128)(2,1)S(1)}, bf16[1,3,128,512]{3,2,1,0:T(8,128)(2,1)}, u32[]{:S(2)}) copy-start(bf16[1,3,128,512]{3,2,1,0:T(8,128)(2,1)} %stash_hbm.1) | copy-start | bytes 1179652
  7.4 0.9 %copy-start.5 = (f32[1,128,512]{2,1,0:T(8,128)S(1)}, f32[1,128,512]{2,1,0:T(8,128)}, u32[]{:S(2)}) copy-start(f32[1,128,512]{2,1,0:T(8,128)} %grad_hbm.1) | copy-start | bytes 786436
  8.4 0.9 %copy-start.6 = (bf16[1,128,512]{2,1,0:T(8,128)(2,1)S(1)}, bf16[1,128,512]{2,1,0:T(8,128)(2,1)}, u32[]{:S(2)}) copy-start(bf16[1,128,512]{2,1,0:T(8,128)(2,1)} %mem_hbm.1) | copy-start | bytes 393220

commit v2 on v1

--- a/solution.py
+++ b/solution.py
@@ -10,7 +10,7 @@
 MESH = pl.DeviceIdType.MESH
 F32 = jnp.float32
 BF16 = jnp.bfloat16
-ORDER = (0, 2, 1, 3)
+ORDER = (0, 1, 2, 3)
 
 
 def nn(a, b):
@@ -28,11 +28,11 @@
 def kernel(
     grad_hbm, mem_hbm, enc_hbm, stash_hbm, slot_ref, len_ref, wq_hbm, wk_hbm, wv_hbm, wo_hbm,
     gout_ref, eout_ref,
-    grad_v, stash_v, wq, wk, wv, wo, held, q_s, k_s, v_s, att, cg_s, sg_s, qg_s, kg_s, vg_s,
+    grad_v, stash_v, wq, wk, wv, wo, held, q_s, k_s, v_s, wot, wqt, att, cg_s, sg_s, kg_s, vg_s,
     gl, gres, dpf, dpb, sibr, r1s, r1r, r2s, r2x, r2y, gfin,
-    mpf, mpb, mpr, cs, cr, fin, esw, esr, encr,
+    mpf, mpb, mpr, cs, cr, fin, encr,
     load_sem, sib_s, sib_r, r1_ss, r1_rs, x_ss, x_rs, y_ss, y_rs, fw_ss, fw_rs,
-    mp_ss, mp_rs, c_ss, c_rs, f_ss, f_rs, h_ss, h_rs, hf_ss, hf_rs, e_ss, e_rs, w_ss, w_rs,
+    mp_ss, mp_rs, c_ss, c_rs, f_ss, f_rs, h_ss, h_rs, hf_ss, hf_rs, e_ss, e_rs,
 ):
     heads = wq.shape[1] // HEAD_DIM
     seg = lax.axis_index("segment")
@@ -83,6 +83,9 @@
     for dev in senders:
         pl.semaphore_signal(barrier, inc=1, device_id=dev, device_id_type=MESH)
 
+    def at(h):
+        return slice(HEAD_DIM * h, HEAD_DIM * h + HEAD_DIM)
+
     def keys_of(t):
         k_s[...] = jnp.concatenate(
             [nn(held[t], wk[:, 256 * n : 256 * n + 256]).astype(BF16) for n in range(4)], axis=1
@@ -101,11 +104,14 @@
 
     def softmax_of(t):
         allowed = lax.broadcasted_iota(jnp.int32, (128, 128), 1) < len_ref[0, t]
+        scores = [nt(q_s[:, at(h)], k_s[:, at(h)]) for h in range(heads)]
+        weights = []
         for h in range(heads):
-            at = slice(HEAD_DIM * h, HEAD_DIM * h + HEAD_DIM)
-            scores = jnp.where(allowed, nt(q_s[:, at], k_s[:, at]), F32(-1e30))
-            expo = jnp.exp(scores - jnp.max(scores, axis=-1, keepdims=True))
-            att[h] = expo / jnp.sum(expo, axis=-1, keepdims=True)
+            score = jnp.where(allowed, scores[h], F32(-1e30))
+            expo = jnp.exp(score - jnp.max(score, axis=-1, keepdims=True))
+            weights.append(expo / jnp.sum(expo, axis=-1, keepdims=True))
+        for h in range(heads):
+            att[h] = weights[h]
 
     loads["mem"].wait()
     loads["wk"].wait()
@@ -139,24 +145,35 @@
     for t in range(TICKS):
         last = t == TICKS - 1
         g = jnp.concatenate([gl[t, j] for j in range(4)], axis=1)
-        for n in range(4):
-            cg_s[:, 256 * n : 256 * n + 256] = nt(g, wo[256 * n : 256 * n + 256, :]).astype(BF16)
+        if t == 0:
+            context = [nt(g, wo[256 * n : 256 * n + 256, :]).astype(BF16) for n in range(4)]
+        else:
+            context = [nn(g, wot[:, 256 * n : 256 * n + 256]).astype(BF16) for n in range(4)]
+        cg_s[...] = jnp.concatenate(context, axis=1)
+        prob_grads = [nt(cg_s[:, at(h)], v_s[:, at(h)]) for h in range(heads)]
+        score_grads = []
         for h in range(heads):
-            at = slice(HEAD_DIM * h, HEAD_DIM * h + HEAD_DIM)
-            prob_grad = nt(cg_s[:, at], v_s[:, at])
             weight = att[h]
-            total = jnp.sum(weight * prob_grad, axis=-1, keepdims=True)
-            score_grad = (weight * (prob_grad - total)).astype(BF16)
-            sg_s[h] = score_grad
-            qg_s[:, at] = nn(score_grad, k_s[:, at]).astype(BF16)
+            total = jnp.sum(weight * prob_grads[h], axis=-1, keepdims=True)
+            score_grads.append((weight * (prob_grads[h] - total)).astype(BF16))
+        query_grads = [nn(score_grads[h], k_s[:, at(h)]).astype(BF16) for h in range(heads)]
+        for h in range(heads):
+            sg_s[h] = score_grads[h]
+        query_grad = jnp.concatenate(query_grads, axis=1)
         pair = {}
-        for j in ORDER:
-            part = nt(qg_s[...], wq[128 * j : 128 * j + 128, :])
-            dpf[j] = part
-            dpb[t, j] = part.astype(BF16)
-            pair[j] = go(
-                rcopy(dpb.at[t, j, other], sibr.at[t, j], sib_s.at[t, j], sib_r.at[t, j], sib)
-            )
+        for n in range(2):
+            cols = slice(256 * n, 256 * n + 256)
+            if t == 0:
+                part = nt(query_grad, wq[cols, :])
+            else:
+                part = nn(query_grad, wqt[:, cols])
+            for j in (2 * n, 2 * n + 1):
+                piece = part[:, 128 * (j - 2 * n) : 128 * (j - 2 * n) + 128]
+                dpf[j] = piece
+                dpb[t, j] = piece.astype(BF16)
+                pair[j] = go(
+                    rcopy(dpb.at[t, j, other], sibr.at[t, j], sib_s.at[t, j], sib_r.at[t, j], sib)
+                )
         first = {}
         for j in ORDER:
             pair[j].wait_recv()
@@ -168,13 +185,13 @@
                     (seg, 2 * partner + k),
                 )
             )
-        for h in range(heads):
-            at = slice(HEAD_DIM * h, HEAD_DIM * h + HEAD_DIM)
-            vg_s[:, at] = tn(att[h].astype(BF16), cg_s[:, at]).astype(BF16)
-            kg_s[:, at] = tn(sg_s[h], q_s[:, at]).astype(BF16)
+        value_grads = [tn(att[h].astype(BF16), cg_s[:, at(h)]).astype(BF16) for h in range(heads)]
+        key_grads = [tn(sg_s[h], q_s[:, at(h)]).astype(BF16) for h in range(heads)]
+        vg_s[...] = jnp.concatenate(value_grads, axis=1)
+        kg_s[...] = jnp.concatenate(key_grads, axis=1)
         for j in range(4):
             rows = slice(128 * j, 128 * j + 128)
-            part = nt(kg_s[...], wk[rows, :]) + nt(vg_s[...], wv[rows, :])
+            part = nt(wk[rows, :], kg_s[...]) + nt(wv[rows, :], vg_s[...])
             mpf[j] = part
             mpb[t, j] = part.astype(BF16)
         mp_copy = go(rcopy(mpb.at[t, :, other], mpr.at[t], mp_ss.at[t], mp_rs.at[t], sib))
@@ -194,6 +211,11 @@
                 rcopy(cs.at[i], cr.at[i], c_ss.at[i], c_rs.at[i], (prev, head))
                 for i in range(TICKS - 1)
             ]
+        if t == 0:
+            for n in range(8):
+                cols = slice(128 * n, 128 * n + 128)
+                wot[:, cols] = wo[cols, :].T
+                wqt[cols, :] = wq[:, cols].T
         if not last:
             helds[t].wait_recv()
             go(held_fw[t])
@@ -235,9 +257,9 @@
         else:
             for r in range(4):
                 final[r].wait_recv()
+            enc_copy.wait_recv()
             total = fin[0].astype(F32) + fin[1].astype(F32) + fin[2].astype(F32) + fin[3].astype(F32)
-            esw[...] = total
-            swap = go(rcopy(esw, esr, w_ss, w_rs, sib))
+            eout_ref[0] = encr[...] + total
         forward = {}
         for j in ORDER:
             straight[j].wait_recv()
@@ -256,14 +278,6 @@
 
     for j in range(4):
         gout_ref[0, :, 128 * j : 128 * j + 128] = gfin[j]
-    swap.wait_recv()
-    enc_copy.wait_recv()
-
-    def my_columns(x):
-        return jnp.where(k == 0, x[:, :64], x[:, 64:])
-
-    eout_ref[0, mine, :] = encr[mine, :] + my_columns(esw[...])
-    eout_ref[0, other, :] = encr[other, :] + my_columns(esr[...])
     for copy in sends:
         copy.wait_send()
 
@@ -287,9 +301,10 @@
         V((512, inner), BF16), V((512, inner), BF16), V((512, inner), BF16), V((inner, 512), BF16),
         V((TICKS, 128, 512), BF16),
         V((128, inner), BF16), V((128, inner), BF16), V((128, inner), BF16),
+        V((512, inner), BF16), V((inner, 512), BF16),
         V((heads, 128, 128), F32),
         V((128, inner), BF16), V((heads, 128, 128), BF16),
-        V((128, inner), BF16), V((128, inner), BF16), V((128, inner), BF16),
+        V((128, inner), BF16), V((128, inner), BF16),
         V((TICKS, 4, 128, 128), BF16), V((4, *half), F32),
         V((4, 128, 128), F32), V((TICKS, 4, 128, 128), BF16), V((TICKS, 4, *half), BF16),
         V((TICKS, 4, *half), BF16), V((TICKS, 4, *half), BF16),
@@ -297,30 +312,32 @@
         V((4, 128, 128), F32),
         V((4, 128, 128), F32), V((TICKS, 4, 128, 128), BF16), V((TICKS, 4, *half), BF16),
         V((TICKS, 4, *half), BF16), V((TICKS - 1, 4, *half), BF16),
-        V((4, *half), BF16), V(half, F32), V(half, F32), V((128, 64), F32),
+        V((4, *half), BF16), V(half, F32),
         dma(7),
         dma(TICKS, 4), dma(TICKS, 4), dma(TICKS, 4), dma(TICKS, 4),
         dma(TICKS, 4), dma(TICKS, 4), dma(TICKS, 4), dma(TICKS, 4), dma(TICKS, 4), dma(TICKS, 4),
         dma(TICKS), dma(TICKS), dma(TICKS - 1), dma(TICKS - 1), dma(4), dma(4),
-        dma(TICKS - 1), dma(TICKS - 1), dma(TICKS - 1), dma(TICKS - 1), dma(), dma(), dma(), dma(),
+        dma(TICKS - 1), dma(TICKS - 1), dma(TICKS - 1), dma(TICKS - 1), dma(), dma(),
     ]
-    return pl.pallas_call(
+    enc_turned = jnp.swapaxes(enc_grad_in, 1, 2)
+    grad_out, enc_out = pl.pallas_call(
         kernel,
         name="relay_backward",
         out_shape=(
             jax.ShapeDtypeStruct(grad_in.shape, F32),
-            jax.ShapeDtypeStruct(enc_grad_in.shape, F32),
+            jax.ShapeDtypeStruct(enc_turned.shape, F32),
         ),
         in_specs=[anywhere] * 4 + [scalars] * 2 + [anywhere] * 4,
         out_specs=(whole, whole),
         scratch_shapes=scratch,
         compiler_params=pltpu.CompilerParams(
-            collective_id=0, has_side_effects=True, vmem_limit_bytes=40 * 1024 * 1024
+            collective_id=0, has_side_effects=True, vmem_limit_bytes=56 * 1024 * 1024
         ),
         cost_estimate=pl.CostEstimate(
             flops=3_400_000_000, bytes_accessed=5_500_000, transcendentals=400_000
         ),
-    )(grad_in, memory, enc_grad_in, act_stash, slot_order, lengths, w_query, w_key, w_value, w_out)
+    )(grad_in, memory, enc_turned, act_stash, slot_order, lengths, w_query, w_key, w_value, w_out)
+    return grad_out, jnp.swapaxes(enc_out, 1, 2)
 
 
 def solution(mesh):

time: 79 us -> 66.9 us (0.85)
  local copies, waits for them, and re-layouts: 10 us -> 2.3 us
  Pallas kernels: 67.8 us -> 63.8 us
    unnamed x20 -> x4, local copies, waits for them, and re-layouts: 9.31 us -> 2.3 us
    pallas_call x1, Pallas kernels: 67.8 us -> 63.8 us  [body(): pl.pallas_call(kernel, name='relay_backward', out_shape=(jax.ShapeDtypeSt...]
where the time goes in v2:
time: 66.9 us; the launch traced here: 66.7 us
  Pallas kernels  63.8 us (95%)
  local copies, waits for them, and re-layouts  2.3 us (3%)
    pallas_call x1, Pallas kernels, body(): pl.pallas_call(kernel, name='relay_backward', out_shape=(jax.ShapeDtypeSt...  63.8 us
    unnamed x4, local copies, waits for them, and re-layouts  2.3 us

profile of v2, /device:TPU:59, one launch (start us, length us, event | category | flops | bytes accessed | tf_op | source)
XLA Modules:
  0.0 66.7 jit_solution(10656690833922174143)
XLA Ops:
  0.6 63.8 %relay_backward.1 = (f32[1,128,512]{2,1,0:T(8,128)}, f32[1,64,128]{2,1,0:T(8,128)}) custom-call(f32[1,128,512]{2,1,0:T(8,128)} %grad_hbm.1, bf16[1,128,512]{2,1,0:T(8,128)(2,1)} %mem_hbm.1, f32[1,64,128]{2,1,0:T(8,128)} %bitcast.3, bf16[1,3,128,512]{3,2,1,0:T(8,128)(2,1)} %stash_hbm.1, s32[1,3]{1,0:T(1,128)} %slot_ref.1, s32[1,3]{1,0:T(1,128)} %len_ref.1, ...), custom_call_target="tpu_custom_call" | custom-call | flops 3400000000 | bytes 5500000 | tf_op jit(solution)/shard_map/relay_backward/pallas_call | solution.py:323
  64.4 0.0 copy-start
  64.4 1.7 %copy.14 = f32[1,128,512]{2,1,0:T(8,128)} copy(f32[1,128,512]{2,1,0:T(8,128)} %get-tuple-element.8) | data formatting | bytes 524288
  66.1 0.0 copy-done
  66.1 0.6 copy.15
Async XLA Ops:
  64.4 1.7 %copy-start = (f32[1,64,128]{2,1,0:T(8,128)S(1)}, f32[1,64,128]{2,1,0:T(8,128)}, u32[]{:S(2)}) copy-start(f32[1,64,128]{2,1,0:T(8,128)} %get-tuple-element.5) | copy-start | bytes 98308

commit v3 on v2

v3 whole, which is shorter than its diff:
```python
import types

import jax
import jax.numpy as jnp
from jax import lax
from jax.experimental import pallas as pl
from jax.experimental.pallas import tpu as pltpu
from jax.sharding import PartitionSpec as P

HEAD_DIM = 128
TICKS = 3
MESH = pl.DeviceIdType.MESH
F32 = jnp.float32
BF16 = jnp.bfloat16
EARLY = ()
FIRST_ORDER = (0, 1, 2, 3)
SECOND_ORDER = (0, 1, 2, 3)


def nn(a, b):
    return lax.dot_general(a, b, (((1,), (0,)), ((), ())), preferred_element_type=F32)


def nt(a, b):
    return lax.dot_general(a, b, (((1,), (1,)), ((), ())), preferred_element_type=F32)


def tn(a, b):
    return lax.dot_general(a, b, (((0,), (0,)), ((), ())), preferred_element_type=F32)


def at(h):
    return slice(HEAD_DIM * h, HEAD_DIM * h + HEAD_DIM)


def wide(a, w):
    return [nn(a, w[:, 256 * n : 256 * n + 256]).astype(BF16) for n in range(w.shape[1] // 256)]


def joined(pieces):
    return jnp.concatenate(pieces, axis=1)


def scratch_spec(inner):
    heads = inner // HEAD_DIM
    half = (64, 128)

    def v(shape, kind):
        return pltpu.VMEM(shape, kind)

    def s(*shape):
        return pltpu.SemaphoreType.DMA(shape) if shape else pltpu.SemaphoreType.DMA

    spec = dict(
        grad=v((128, 512), F32), stash=v((TICKS, 128, 512), BF16),
        wq=v((512, inner), BF16), wk=v((512, inner), BF16), wv=v((512, inner), BF16),
        wo=v((inner, 512), BF16), wot=v((2, 512, inner), BF16), wqt=v((2, inner, 512), BF16),
        wk2=v((512, inner), BF16), wv2=v((512, inner), BF16),
        held=v((TICKS, 128, 512), BF16),
        q=v((TICKS, 128, inner), BF16), k=v((TICKS, 2, 128, inner), BF16),
        v=v((TICKS, 2, 128, inner), BF16), q2=v((TICKS, 64, inner), BF16),
        att=v((heads, 128, 128), F32), att2=v((2 * heads, 64, 128), F32),
        cg=v((128, inner), BF16), sg=v((heads, 128, 128), BF16),
        cg2=v((2, 64, inner), BF16), cgf=v((2, 64, inner), F32), sg2=v((2 * heads, 64, 128), BF16),
        kg=v((2, 128, inner), BF16), vg=v((2, 128, inner), BF16),
        gres=v((8, 32, 128), F32), dpf=v((4, 128, 128), F32), dpb=v((4, 128, 128), BF16),
        sibr=v((4, *half), BF16),
        r1s=v((TICKS, 8, 32, 128), BF16), r1r=v((TICKS, 8, 32, 128), BF16),
        r2s=v((TICKS, 8, 32, 128), BF16), r2x=v((TICKS, 8, 32, 128), BF16),
        r2y=v((TICKS, 8, 32, 128), BF16), gfin=v((4, *half), F32),
        mpf=v((4, 128, 128), F32), mpb=v((TICKS, 4, 128, 128), BF16),
        mpr=v((TICKS, 4, *half), BF16), cs=v((TICKS, 4, *half), BF16),
        cr=v((TICKS - 1, 4, *half), BF16), fin=v((4, *half), BF16), encr=v(half, F32),
        load=s(7),
    )
    for name, shape in dict(
        sib=(4,), r1=(TICKS, 8), x=(TICKS, 8), y=(TICKS, 8), fw=(4,), mp=(TICKS,), c=(TICKS - 1,),
        f=(4,), h=(TICKS - 1,), hf=(TICKS - 1,), e=(), w=(4,), kk=(TICKS,), vv=(TICKS,), qq=(TICKS,),
    ).items():
        spec[name + "_ss"] = s(*shape)
        spec[name + "_rs"] = s(*shape)
    return spec


def kernel(
    names, grad_hbm, mem_hbm, enc_hbm, stash_hbm, slot_ref, len_ref, wq_hbm, wk_hbm, wv_hbm, wo_hbm,
    gout_ref, eout_ref, *scratch
):
    z = types.SimpleNamespace(**dict(zip(names, scratch)))
    heads = z.wq.shape[1] // HEAD_DIM
    seg = lax.axis_index("segment")
    head = lax.axis_index("head")
    segments = lax.axis_size("segment")
    c = head // 2
    k = head % 2
    prev = (seg + segments - 1) % segments
    prev3 = (seg + 3 * segments - 3) % segments
    nxt = (seg + 1) % segments
    nxt3 = (seg + 3) % segments
    c1 = c + 1 - 2 * (c % 2)
    c3 = 3 - c
    sib = (seg, 2 * c + 1 - k)
    mine = pl.ds(pl.multiple_of(64 * k, 64), 64)
    other = pl.ds(pl.multiple_of(64 * (1 - k), 64), 64)

    def rcopy(src, dst, ss, rs, dev):
        return pltpu.make_async_remote_copy(
            src_ref=src, dst_ref=dst, send_sem=ss, recv_sem=rs, device_id=dev, device_id_type=MESH
        )

    sends = []

    def go(copy):
        copy.start()
        sends.append(copy)
        return copy

    loads = {}

    def load(name, src, dst):
        copy = pltpu.make_async_copy(src, dst, z.load.at[len(loads)])
        copy.start()
        loads[name] = copy

    load("mem", mem_hbm.at[0], z.held.at[0])
    load("wk", wk_hbm.at[0], z.wk)
    load("stash", stash_hbm.at[0], z.stash)
    load("wq", wq_hbm.at[0], z.wq)
    load("wv", wv_hbm.at[0], z.wv)
    load("grad", grad_hbm.at[0], z.grad)
    load("wo", wo_hbm.at[0], z.wo)

    barrier = pltpu.get_barrier_semaphore()
    senders = [sib, (seg, 2 * c1 + k), (seg, 2 * c3 + k), (nxt3, head)]
    senders += [(nxt, 2 * ((c + r) % 4) + k) for r in range(4)]
    for dev in senders:
        pl.semaphore_signal(barrier, inc=1, device_id=dev, device_id_type=MESH)

    def keys_of(t):
        z.k[t, 0] = joined(wide(z.held[t], z.wk))

    def values_of(t):
        z.v[t, 0] = joined(wide(z.held[t], z.wv))

    def queries_of(t):
        z.q[t] = joined(wide(z.stash[slot_ref[0, t]], z.wq))

    def softmax_of(t, scores, out):
        allowed = lax.broadcasted_iota(jnp.int32, scores[0].shape, 1) < len_ref[0, t]
        weights = []
        for score in scores:
            score = jnp.where(allowed, score, F32(-1e30))
            expo = jnp.exp(score - jnp.max(score, axis=-1, keepdims=True))
            weights.append(expo / jnp.sum(expo, axis=-1, keepdims=True))
        for h, weight in enumerate(weights):
            out[h] = weight

    loads["mem"].wait()
    loads["wk"].wait()
    keys_of(0)
    loads["stash"].wait()
    loads["wq"].wait()
    queries_of(0)

    pl.semaphore_wait(barrier, 8)
    helds = [
        rcopy(z.held.at[t, mine], z.held.at[t + 1, mine], z.h_ss.at[t], z.h_rs.at[t], (prev, head))
        for t in range(TICKS - 1)
    ]
    held_fw = [
        rcopy(z.held.at[t + 1, mine], z.held.at[t + 1, mine], z.hf_ss.at[t], z.hf_rs.at[t], sib)
        for t in range(TICKS - 1)
    ]
    go(helds[0])
    enc_copy = go(rcopy(enc_hbm.at[0], z.encr, z.e_ss, z.e_rs, (prev3, head)))

    softmax_of(0, [nt(z.q[0, :, at(h)], z.k[0, 0, :, at(h)]) for h in range(heads)], z.att)
    loads["wv"].wait()
    values_of(0)
    loads["grad"].wait()
    for j in range(4):
        for u in range(2):
            rows = pl.ds(pl.multiple_of(64 * k + 32 * u, 32), 32)
            z.gres[2 * j + u] = z.grad[rows, 128 * j : 128 * j + 128]
    loads["wo"].wait()

    def keeps(j):
        if j in EARLY:
            side = c
        else:
            side = (c // 2) if (j // 2) % 2 == 0 else ((c + 1) // 2) % 2
        return jnp.where(side == 0, F32(1.0), F32(0.0))

    def partners(j):
        return (c1, c3) if (j // 2) % 2 == 0 else (c3, c1)

    def first_round(t, j, total, first, straight):
        partner = partners(j)[0]
        if j in EARLY:
            total = total + keeps(j) * z.gres[j]
        z.r1s[t, j] = total.astype(BF16)
        section = prev if j in EARLY else seg
        first[j] = go(
            rcopy(
                z.r1s.at[t, j], z.r1r.at[t, j], z.r1_ss.at[t, j], z.r1_rs.at[t, j],
                (section, 2 * partner + k),
            )
        )
        if j in EARLY:
            straight[j] = go(
                rcopy(z.r1s.at[t, j], z.r2x.at[t, j], z.x_ss.at[t, j], z.x_rs.at[t, j], (prev, head))
            )

    def second_round(t, j, first, straight, across):
        partner = partners(j)[1]
        first[j].wait_recv()
        if j in EARLY:
            straight[j].wait_recv()
            total = z.r2x[t, j].astype(F32) + z.r1r[t, j].astype(F32)
        else:
            total = z.r1s[t, j].astype(F32) + z.r1r[t, j].astype(F32) + keeps(j) * z.gres[j]
        z.r2s[t, j] = total.astype(BF16)
        section = seg if j in EARLY else prev
        across[j] = go(
            rcopy(
                z.r2s.at[t, j], z.r2y.at[t, j], z.y_ss.at[t, j], z.y_rs.at[t, j],
                (section, 2 * partner + k),
            )
        )
        if j not in EARLY:
            straight[j] = go(
                rcopy(z.r2s.at[t, j], z.r2x.at[t, j], z.x_ss.at[t, j], z.x_rs.at[t, j], (prev, head))
            )

    def gathered(t, j, straight, across):
        across[j].wait_recv()
        if j in EARLY:
            return z.r2s[t, j].astype(F32) + z.r2y[t, j].astype(F32)
        straight[j].wait_recv()
        return z.r2x[t, j].astype(F32) + z.r2y[t, j].astype(F32)

    weight_copies = []
    shared = None
    for t in range(TICKS):
        last = t == TICKS - 1
        first, straight, across = {}, {}, {}
        if t == 0:
            g = z.grad[...].astype(BF16)
            z.cg[...] = joined(
                [nt(g, z.wo[256 * n : 256 * n + 256, :]).astype(BF16) for n in range(4)]
            )
            prob_grads = [nt(z.cg[:, at(h)], z.v[0, 0, :, at(h)]) for h in range(heads)]
            score_grads = []
            for h in range(heads):
                weight = z.att[h]
                total = jnp.sum(weight * prob_grads[h], axis=-1, keepdims=True)
                score_grads.append((weight * (prob_grads[h] - total)).astype(BF16))
            query_grad = joined(
                [nn(score_grads[h], z.k[0, 0, :, at(h)]).astype(BF16) for h in range(heads)]
            )
            for h in range(heads):
                z.sg[h] = score_grads[h]
            pair = {}
            for n in range(2):
                part = nt(query_grad, z.wq[256 * n : 256 * n + 256, :])
                for j in (2 * n, 2 * n + 1):
                    piece = part[:, 128 * (j - 2 * n) : 128 * (j - 2 * n) + 128]
                    z.dpf[j] = piece
                    z.dpb[j] = piece.astype(BF16)
                    pair[j] = go(
                        rcopy(z.dpb.at[j, other], z.sibr.at[j], z.sib_ss.at[j], z.sib_rs.at[j], sib)
                    )
            for j in FIRST_ORDER:
                pair[j].wait_recv()
                total = z.dpf[j, mine] + z.sibr[j].astype(F32)
                for u in range(2):
                    first_round(t, 2 * j + u, total[32 * u : 32 * u + 32], first, straight)
        else:
            shared[1].wait_recv()
            both = [(h // heads, h % heads) for h in range(2 * heads)]
            prob_grads = [nt(z.cg2[i, :, at(h)], z.v[t, i, :, at(h)]) for i, h in both]
            score_grads = []
            for i, h in both:
                weight = z.att2[heads * i + h]
                total = jnp.sum(weight * prob_grads[heads * i + h], axis=-1, keepdims=True)
                score_grads.append((weight * (prob_grads[heads * i + h] - total)).astype(BF16))
            query_grads = [
                nn(score_grads[heads * i + h], z.k[t, i, :, at(h)]).astype(BF16) for i, h in both
            ]
            for h in range(2 * heads):
                z.sg2[h] = score_grads[h]
            query_grad = [joined(query_grads[:heads]), joined(query_grads[heads:])]
            if t == 1:
                weight_copies[1].wait_recv()
            for n in range(2):
                cols = slice(256 * n, 256 * n + 256)
                part = nn(query_grad[0], z.wqt[0, :, cols]) + nn(query_grad[1], z.wqt[1, :, cols])
                for j in (2 * n, 2 * n + 1):
                    piece = part[:, 128 * (j - 2 * n) : 128 * (j - 2 * n) + 128]
                    for u in range(2):
                        first_round(t, 2 * j + u, piece[32 * u : 32 * u + 32], first, straight)
        if t == 0:
            vgs = [tn(z.att[h].astype(BF16), z.cg[:, at(h)]).astype(BF16) for h in range(heads)]
            kgs = [tn(z.sg[h], z.q[0, :, at(h)]).astype(BF16) for h in range(heads)]
            z.vg[0] = joined(vgs)
            z.kg[0] = joined(kgs)
        else:
            vgs = [
                tn(z.att2[heads * i + h].astype(BF16), z.cg2[i, :, at(h)]).astype(BF16)
                for i, h in both
            ]
            kgs = [
                tn(z.sg2[heads * i + h], z.q[t, mine, at(h)] if i == 0 else z.q2[t, :, at(h)]).astype(
                    BF16
                )
                for i, h in both
            ]
            for i in range(2):
                z.vg[i] = joined(vgs[heads * i : heads * i + heads])
                z.kg[i] = joined(kgs[heads * i : heads * i + heads])
            if t == 1:
                weight_copies[2].wait_recv()
                weight_copies[3].wait_recv()
        for j in range(4):
            rows = slice(128 * j, 128 * j + 128)
            part = nt(z.wk[rows, :], z.kg[0]) + nt(z.wv[rows, :], z.vg[0])
            if t > 0:
                part = part + nt(z.wk2[rows, :], z.kg[1]) + nt(z.wv2[rows, :], z.vg[1])
            z.mpf[j] = part
            z.mpb[t, j] = part.astype(BF16)
        mp_copy = go(rcopy(z.mpb.at[t, :, other], z.mpr.at[t], z.mp_ss.at[t], z.mp_rs.at[t], sib))
        if t == 0:
            for n in range(8):
                z.wot[0, :, at(n)] = z.wo[at(n), :].T
            weight_copies.append(
                go(rcopy(z.wot.at[0], z.wot.at[1], z.w_ss.at[0], z.w_rs.at[0], sib))
            )
            for n in range(8):
                z.wqt[0, at(n), :] = z.wq[:, at(n)].T
            weight_copies.append(
                go(rcopy(z.wqt.at[0], z.wqt.at[1], z.w_ss.at[1], z.w_rs.at[1], sib))
            )
        if not last:
            helds[t].wait_recv()
            go(held_fw[t])
            if t + 1 < TICKS - 1:
                go(helds[t + 1])
            n = t + 1
            queries_of(n)
            queries = rcopy(z.q.at[n, other], z.q2.at[n], z.qq_ss.at[n], z.qq_rs.at[n], sib)
            go(queries)
            held_fw[t].wait_recv()
            keys_of(n)
            shared = [
                go(rcopy(z.k.at[n, 0], z.k.at[n, 1], z.kk_ss.at[n], z.kk_rs.at[n], sib)),
                rcopy(z.v.at[n, 0], z.v.at[n, 1], z.vv_ss.at[n], z.vv_rs.at[n], sib),
            ]
        if t == 0:
            carried = [
                rcopy(z.cs.at[i], z.cr.at[i], z.c_ss.at[i], z.c_rs.at[i], (prev, head))
                for i in range(TICKS - 1)
            ]
        mp_copy.wait_recv()
        if t > 0:
            carried[t - 1].wait_recv()
        for j in range(4):
            part = z.mpf[j, mine] + z.mpr[t, j].astype(F32)
            if t > 0:
                part = part + z.cr[t - 1, j].astype(F32)
            z.cs[t, j] = part.astype(BF16)
        if last:
            final = []
            for r in range(4):
                dest = (c + r) % 4
                final.append(
                    go(
                        rcopy(
                            z.cs.at[t, dest], z.fin.at[r], z.f_ss.at[r], z.f_rs.at[r],
                            (prev, 2 * dest + k),
                        )
                    )
                )
        for j in SECOND_ORDER:
            for u in range(2):
                second_round(t, 2 * j + u, first, straight, across)
        if not last:
            go(carried[t])
        if t == 0:
            for i, (src, dst) in enumerate(((z.wk, z.wk2), (z.wv, z.wv2))):
                weight_copies.append(go(rcopy(src, dst, z.w_ss.at[2 + i], z.w_rs.at[2 + i], sib)))
        if not last:
            values_of(n)
            go(shared[1])
            scores = [nt(z.q[n, mine, at(h)], z.k[n, 0, :, at(h)]) for h in range(heads)]
            queries.wait_recv()
            shared[0].wait_recv()
            scores += [nt(z.q2[n, :, at(h)], z.k[n, 1, :, at(h)]) for h in range(heads)]
            softmax_of(n, scores, z.att2)
            if t == 0:
                weight_copies[0].wait_recv()
            for pair in (SECOND_ORDER[:2], SECOND_ORDER[2:]):
                pieces = []
                for j in pair:
                    totals = []
                    for u in range(2):
                        totals.append(gathered(t, 2 * j + u, straight, across))
                        z.gres[2 * j + u] = totals[u]
                    pieces.append(jnp.concatenate(totals, axis=0).astype(BF16))
                g = joined(pieces)
                for i in range(2):
                    for m in range(z.cgf.shape[2] // 256):
                        cols = slice(256 * m, 256 * m + 256)
                        w = jnp.concatenate([z.wot[i, at(j), cols] for j in pair], axis=0)
                        part = nn(g, w)
                        if pair == SECOND_ORDER[:2]:
                            z.cgf[i, :, cols] = part
                        else:
                            z.cg2[i, :, cols] = (z.cgf[i, :, cols] + part).astype(BF16)
        else:
            forward = {}
            for j in SECOND_ORDER:
                cols = slice(128 * j, 128 * j + 128)
                gout_ref[0, mine, cols] = jnp.concatenate(
                    [gathered(t, 2 * j + u, straight, across) for u in range(2)], axis=0
                )
                forward[j] = go(
                    rcopy(
                        gout_ref.at[0, mine, cols], z.gfin.at[j], z.fw_ss.at[j], z.fw_rs.at[j], sib
                    )
                )
            for r in range(4):
                final[r].wait_recv()
            enc_copy.wait_recv()
            eout_ref[0] = (
                z.encr[...]
                + (z.fin[0].astype(F32) + z.fin[1].astype(F32))
                + (z.fin[2].astype(F32) + z.fin[3].astype(F32))
            )
            for j in SECOND_ORDER:
                forward[j].wait_recv()
                gout_ref[0, other, 128 * j : 128 * j + 128] = z.gfin[j]

    for copy in sends:
        copy.wait_send()


def body(
    grad_in, memory, enc_grad_in, act_stash, slot_order, lengths, w_query, w_key, w_value, w_out
):
    anywhere = pl.BlockSpec(memory_space=pl.ANY)
    scalars = pl.BlockSpec(memory_space=pltpu.SMEM)
    whole = pl.BlockSpec(memory_space=pltpu.VMEM)
    spec = scratch_spec(w_query.shape[2])
    names = tuple(spec)
    enc_turned = jnp.swapaxes(enc_grad_in, 1, 2)

    def relay(*refs):
        kernel(names, *refs)

    grad_out, enc_out = pl.pallas_call(
        relay,
        name="relay_backward",
        out_shape=(
            jax.ShapeDtypeStruct(grad_in.shape, F32),
            jax.ShapeDtypeStruct(enc_turned.shape, F32),
        ),
        in_specs=[anywhere] * 4 + [scalars] * 2 + [anywhere] * 4,
        out_specs=(whole, whole),
        scratch_shapes=list(spec.values()),
        compiler_params=pltpu.CompilerParams(
            collective_id=0, has_side_effects=True, vmem_limit_bytes=56 * 1024 * 1024
        ),
        cost_estimate=pl.CostEstimate(
            flops=3_400_000_000, bytes_accessed=5_500_000, transcendentals=400_000
        ),
    )(grad_in, memory, enc_turned, act_stash, slot_order, lengths, w_query, w_key, w_value, w_out)
    return grad_out, jnp.swapaxes(enc_out, 1, 2)


def solution(mesh):
    in_specs = (
        P("segment", None, None),
        P("segment", None, None),
        P("segment", None, "head"),
        P("segment", None, None, None),
        P("segment", None),
        P("segment", None),
        P("segment", None, "head"),
        P("segment", None, "head"),
        P("segment", None, "head"),
        P("segment", "head", None),
    )
    out_specs = (P("segment", None, None), P("segment", None, "head"))
    return jax.shard_map(body, mesh=mesh, in_specs=in_specs, out_specs=out_specs, check_vma=False)
```

time: 66.9 us -> 65.9 us (0.985)
  Pallas kernels: 63.8 us -> 62.7 us
    pallas_call x1, Pallas kernels: 63.8 us -> 62.7 us  [body(): pl.pallas_call(relay, name='relay_backward', out_shape=(jax.ShapeDtypeStr...]
where the time goes in v3:
time: 65.9 us; the launch traced here: 65.7 us
  Pallas kernels  62.7 us (95%)
  local copies, waits for them, and re-layouts  2.3 us (3%)
    pallas_call x1, Pallas kernels, body(): pl.pallas_call(relay, name='relay_backward', out_shape=(jax.ShapeDtypeStr...  62.7 us
    unnamed x4, local copies, waits for them, and re-layouts  2.3 us

profile of v3, /device:TPU:59, one launch (start us, length us, event | category | flops | bytes accessed | tf_op | source)
XLA Modules:
  0.0 65.7 jit_solution(13715985303698867419)
XLA Ops:
  0.6 62.7 %relay_backward.1 = (f32[1,128,512]{2,1,0:T(8,128)}, f32[1,64,128]{2,1,0:T(8,128)}) custom-call(f32[1,128,512]{2,1,0:T(8,128)} %refs_0_.1, bf16[1,128,512]{2,1,0:T(8,128)(2,1)} %refs_1_.1, f32[1,64,128]{2,1,0:T(8,128)} %bitcast.3, bf16[1,3,128,512]{3,2,1,0:T(8,128)(2,1)} %refs_3_.1, s32[1,3]{1,0:T(1,128)} %refs_4_.1, s32[1,3]{1,0:T(1,128)} %refs_5_.1, ...), custom_call_target="tpu_custom_call" | custom-call | flops 3400000000 | bytes 5500000 | tf_op jit(solution)/shard_map/relay_backward/pallas_call | solution.py:460
  63.4 0.0 copy-start
  63.4 1.7 %copy.14 = f32[1,128,512]{2,1,0:T(8,128)} copy(f32[1,128,512]{2,1,0:T(8,128)} %get-tuple-element.8) | data formatting | bytes 524288
  65.1 0.0 copy-done
  65.1 0.6 copy.15
Async XLA Ops:
  63.4 1.7 %copy-start = (f32[1,64,128]{2,1,0:T(8,128)S(1)}, f32[1,64,128]{2,1,0:T(8,128)}, u32[]{:S(2)}) copy-start(f32[1,64,128]{2,1,0:T(8,128)} %get-tuple-element.5) | copy-start | bytes 98308

commit v4 on v3

--- a/solution.py
+++ b/solution.py
@@ -162,7 +162,6 @@
     loads["wq"].wait()
     queries_of(0)
 
-    pl.semaphore_wait(barrier, 8)
     helds = [
         rcopy(z.held.at[t, mine], z.held.at[t + 1, mine], z.h_ss.at[t], z.h_rs.at[t], (prev, head))
         for t in range(TICKS - 1)
@@ -171,8 +170,7 @@
         rcopy(z.held.at[t + 1, mine], z.held.at[t + 1, mine], z.hf_ss.at[t], z.hf_rs.at[t], sib)
         for t in range(TICKS - 1)
     ]
-    go(helds[0])
-    enc_copy = go(rcopy(enc_hbm.at[0], z.encr, z.e_ss, z.e_rs, (prev3, head)))
+    enc_copy = rcopy(enc_hbm.at[0], z.encr, z.e_ss, z.e_rs, (prev3, head))
 
     softmax_of(0, [nt(z.q[0, :, at(h)], z.k[0, 0, :, at(h)]) for h in range(heads)], z.att)
     loads["wv"].wait()
@@ -260,16 +258,20 @@
             )
             for h in range(heads):
                 z.sg[h] = score_grads[h]
-            pair = {}
             for n in range(2):
                 part = nt(query_grad, z.wq[256 * n : 256 * n + 256, :])
                 for j in (2 * n, 2 * n + 1):
                     piece = part[:, 128 * (j - 2 * n) : 128 * (j - 2 * n) + 128]
                     z.dpf[j] = piece
                     z.dpb[j] = piece.astype(BF16)
-                    pair[j] = go(
-                        rcopy(z.dpb.at[j, other], z.sibr.at[j], z.sib_ss.at[j], z.sib_rs.at[j], sib)
-                    )
+            pl.semaphore_wait(barrier, 8)
+            pair = {}
+            for j in FIRST_ORDER:
+                pair[j] = go(
+                    rcopy(z.dpb.at[j, other], z.sibr.at[j], z.sib_ss.at[j], z.sib_rs.at[j], sib)
+                )
+            go(helds[0])
+            go(enc_copy)
             for j in FIRST_ORDER:
                 pair[j].wait_recv()
                 total = z.dpf[j, mine] + z.sibr[j].astype(F32)
@@ -341,20 +343,20 @@
                 go(rcopy(z.wqt.at[0], z.wqt.at[1], z.w_ss.at[1], z.w_rs.at[1], sib))
             )
         if not last:
-            helds[t].wait_recv()
-            go(held_fw[t])
-            if t + 1 < TICKS - 1:
-                go(helds[t + 1])
             n = t + 1
             queries_of(n)
             queries = rcopy(z.q.at[n, other], z.q2.at[n], z.qq_ss.at[n], z.qq_rs.at[n], sib)
+            if t > 0:
+                helds[t].wait_recv()
+                go(held_fw[t])
             go(queries)
-            held_fw[t].wait_recv()
-            keys_of(n)
-            shared = [
-                go(rcopy(z.k.at[n, 0], z.k.at[n, 1], z.kk_ss.at[n], z.kk_rs.at[n], sib)),
-                rcopy(z.v.at[n, 0], z.v.at[n, 1], z.vv_ss.at[n], z.vv_rs.at[n], sib),
-            ]
+            if t > 0:
+                held_fw[t].wait_recv()
+                keys_of(n)
+                shared = [
+                    go(rcopy(z.k.at[n, 0], z.k.at[n, 1], z.kk_ss.at[n], z.kk_rs.at[n], sib)),
+                    rcopy(z.v.at[n, 0], z.v.at[n, 1], z.vv_ss.at[n], z.vv_rs.at[n], sib),
+                ]
         if t == 0:
             carried = [
                 rcopy(z.cs.at[i], z.cr.at[i], z.c_ss.at[i], z.c_rs.at[i], (prev, head))
@@ -380,6 +382,9 @@
                         )
                     )
                 )
+        if t == 0:
+            helds[t].wait_recv()
+            go(held_fw[t])
         for j in SECOND_ORDER:
             for u in range(2):
                 second_round(t, 2 * j + u, first, straight, across)
@@ -389,6 +394,15 @@
             for i, (src, dst) in enumerate(((z.wk, z.wk2), (z.wv, z.wv2))):
                 weight_copies.append(go(rcopy(src, dst, z.w_ss.at[2 + i], z.w_rs.at[2 + i], sib)))
         if not last:
+            if n < TICKS - 1:
+                go(helds[n])
+            if t == 0:
+                held_fw[t].wait_recv()
+                keys_of(n)
+                shared = [
+                    go(rcopy(z.k.at[n, 0], z.k.at[n, 1], z.kk_ss.at[n], z.kk_rs.at[n], sib)),
+                    rcopy(z.v.at[n, 0], z.v.at[n, 1], z.vv_ss.at[n], z.vv_rs.at[n], sib),
+                ]
             values_of(n)
             go(shared[1])
             scores = [nt(z.q[n, mine, at(h)], z.k[n, 0, :, at(h)]) for h in range(heads)]

time: 65.9 us -> 65.4 us (level)
  no operation moved by 1% of the time
where the time goes in v4:
time: 65.4 us; the launch traced here: 65.2 us
  Pallas kernels  62.3 us (95%)
  local copies, waits for them, and re-layouts  2.3 us (4%)
    pallas_call x1, Pallas kernels, body(): pl.pallas_call(relay, name='relay_backward', out_shape=(jax.ShapeDtypeStr...  62.3 us
    unnamed x4, local copies, waits for them, and re-layouts  2.3 us

profile of v4, /device:TPU:59, one launch (start us, length us, event | category | flops | bytes accessed | tf_op | source)
XLA Modules:
  0.0 65.2 jit_solution(4762339007955069123)
XLA Ops:
  0.6 62.3 %relay_backward.1 = (f32[1,128,512]{2,1,0:T(8,128)}, f32[1,64,128]{2,1,0:T(8,128)}) custom-call(f32[1,128,512]{2,1,0:T(8,128)} %refs_0_.1, bf16[1,128,512]{2,1,0:T(8,128)(2,1)} %refs_1_.1, f32[1,64,128]{2,1,0:T(8,128)} %bitcast.3, bf16[1,3,128,512]{3,2,1,0:T(8,128)(2,1)} %refs_3_.1, s32[1,3]{1,0:T(1,128)} %refs_4_.1, s32[1,3]{1,0:T(1,128)} %refs_5_.1, ...), custom_call_target="tpu_custom_call" | custom-call | flops 3400000000 | bytes 5500000 | tf_op jit(solution)/shard_map/relay_backward/pallas_call | solution.py:474
  62.9 0.0 copy-start
  62.9 1.7 %copy.14 = f32[1,128,512]{2,1,0:T(8,128)} copy(f32[1,128,512]{2,1,0:T(8,128)} %get-tuple-element.8) | data formatting | bytes 524288
  64.6 0.0 copy-done
  64.6 0.6 copy.15
Async XLA Ops:
  62.9 1.7 %copy-start = (f32[1,64,128]{2,1,0:T(8,128)S(1)}, f32[1,64,128]{2,1,0:T(8,128)}, u32[]{:S(2)}) copy-start(f32[1,64,128]{2,1,0:T(8,128)} %get-tuple-element.5) | copy-start | bytes 98308
